TPU v7x, 512 devices: a whole 4x4x16 slice. The times are simulated.
512 devices in a mesh: wide: 64 (over y, z_lo, core), narrow: 8 (over z_hi, x).
Axes of the slice: x: 4, y: 4, z: 16 (z_hi: 2, z_lo: 8; z = z_hi * 8 + z_lo), core: 2. Of those that a mesh axis runs over, the one named last changes fastest.
Arguments:
- spin: float32 [3, 32, 128, 1024], P(None, None, 'wide', 'narrow'), may hold values from -1 to 1, as said below
- region: int32 [32, 128, 1024], P(None, 'wide', 'narrow'), may hold values 0 or 1
- material: int32 [32, 128, 1024], P(None, 'wide', 'narrow'), may hold values from 0 to 3
- saturation: float32 [4], replicated, may hold values from 0.5 to 2
- anisotropy: float32 [4], replicated, may hold values from 0.2 to 1
- damping: float32 [4], replicated, may hold values from 0.05 to 0.5
- applied: float32 [3], replicated, may hold values from -3 to 3
- demag_spectrum: bfloat16 [6, 64, 256, 2048], P(None, 'wide', 'narrow'), may hold values from -2.5 to 2.5, as said below
Outputs:
- rate: float32 [3, 32, 128, 1024], P(None, None, 'wide', 'narrow')
- demag_field: float32 [3, 32, 128, 1024], P(None, None, 'wide', 'narrow')
Inputs may be any that keep to these rules, and one draw needn't show every extreme that they name: `spin`: every cell's three components form a unit vector. `demag_spectrum`: every component is unchanged when all three wave numbers are replaced by their negatives modulo 64, 256, 2048.
All inputs are finite; a program needn't handle non-finite values. No bound on the sum of `region` on one device may be relied on, other than what follows from the above.
Results may differ from a plain program's by a relative error of at most 0.0003.
Values sent between devices are 32-bit elements; how exact they have to be, the bound alone decides.
A program may use at most 64 MiB of HBM per device.

v0:
```python
import functools
import math

import jax
import jax.numpy as jnp
import ml_dtypes
import numpy as np
from jax import lax
from jax.experimental import pallas as pl
from jax.experimental.pallas import tpu as pltpu
from jax.sharding import PartitionSpec as P

EXCHANGE = 0.3
MESH = pl.DeviceIdType.MESH
WIDE, NARROW = 64, 8
NZ, LZ, NX, LX, NY, LY = 32, 64, 128, 256, 1024, 2048
ROWS = 16
GROUP = 2 * NARROW
LANES = 128
HALF = 64
MSG = 6 * LANES
F32, BF16 = jnp.float32, jnp.bfloat16


def halves(x):
    hi = x.astype(np.float32).astype(ml_dtypes.bfloat16)
    lo = (x - hi.astype(np.float64)).astype(ml_dtypes.bfloat16)
    return hi, lo


def slots():
    row = np.arange(WIDE)
    return np.where(row <= 32, row % 32, WIDE - row)


def z_forward():
    s, z = slots()[:, None], np.arange(NZ)[None]
    angle = 2 * np.pi * (s * z % LZ) / LZ
    re = np.cos(angle)
    im = np.where(s == 0, np.where(z % 2, -1.0, 1.0), -np.sin(angle))
    return np.concatenate([re, im], 0)


def z_inverse():
    parts = z_forward().reshape(2, 2, 32, NZ)
    return parts.transpose(3, 1, 0, 2).reshape(NZ, 128)


def x_order():
    return np.arange(NX).reshape(WIDE, 2).T.reshape(-1)


def kx_rows():
    start = 32 * np.arange(NARROW)[:, None]
    return np.concatenate([(start + np.arange(ROWS)[None]).reshape(-1), start[:, 0] + ROWS])


def x_forward():
    kx = kx_rows()
    angle = 2 * np.pi * (kx[:, None] * x_order()[None] % LX) / LX
    return np.concatenate([np.cos(angle), -np.sin(angle)], 1)


def x_inverse():
    kx = kx_rows()
    weight = np.where(kx % 16 == 0, 1.0, 2.0) / (LZ * LX * LY)
    angle = 2 * np.pi * (x_order()[:, None] * kx[None] % LX) / LX
    return np.concatenate([np.cos(angle) * weight, np.sin(angle) * weight], 1)


def y_inner(sign):
    p = np.arange(HALF)
    angle = sign * 2 * np.pi * (p[:, None] * p[None] % HALF) / HALF
    c, s = np.cos(angle), np.sin(angle)
    return np.block([[c, s], [-s, c]])


def y_twist():
    k, p = np.arange(32)[:, None], np.arange(HALF)[None]
    angle = -2 * np.pi * (k * p) / LY
    c, s = np.cos(angle), np.sin(angle)
    both = np.stack([np.concatenate([c, c], 1), np.concatenate([-s, s], 1)])
    return both.astype(np.float32)


DIAGONALS = ((0, 1, 2), (3, 5, 4), (4, 3, 5))
ROWS_OF = ((0, 3, 4), (3, 1, 5), (4, 5, 2))


def mm(a, b):
    dot = functools.partial(jnp.dot, preferred_element_type=F32)
    return dot(a[0], b[0]) + (dot(a[0], b[1]) + dot(a[1], b[0]))


def split(x):
    hi = x.astype(BF16)
    return hi, (x - hi.astype(F32)).astype(BF16)


def tiles(x):
    return [x[:, i:i + LANES] for i in range(0, x.shape[1], LANES)]


def swap(x):
    return jnp.concatenate([pltpu.roll(t, HALF, 1) for t in tiles(x)], 1)


def low_half(shape):
    return (lax.broadcasted_iota(jnp.int32, shape, 1) & (LANES - 1)) < HALF


def sign_of(shape):
    return jnp.where(low_half(shape), -1.0, 1.0).astype(F32)


def turn(v, angle, sign):
    c, s = math.cos(angle), math.sin(angle)
    if abs(s) < 1e-9 and c > 0:
        return v
    j = pltpu.roll(v, HALF, 1) * sign
    if abs(c) < 1e-9:
        return j if s > 0 else -j
    if abs(c - s) < 1e-9:
        return (v + j) * c
    if abs(c + s) < 1e-9:
        return (v - j) * c
    return v * c + j * s


def fft(values, direction, sign):
    n = len(values)
    if n == 1:
        return values
    even = fft(values[0::2], direction, sign)
    odd = fft(values[1::2], direction, sign)
    odd = [turn(o, direction * 2 * math.pi * k / n, sign) for k, o in enumerate(odd)]
    return [e + o for e, o in zip(even, odd)] + [e - o for e, o in zip(even, odd)]


def shifted(x, step):
    zero = jnp.zeros((1, x.shape[1]), x.dtype)
    if step > 0:
        return jnp.concatenate([x[1:], zero], 0)
    return jnp.concatenate([zero, x[:-1]], 0)


def kernel(spin, region, material, satur, aniso, damp, applied, demag_spec,
           zf_hi, zf_lo, zi_hi, zi_lo, xf_hi, xf_lo, xi_hi, xi_lo,
           wf_hi, wf_lo, wi_hi, wi_lo, twist,
           rate_out, demag_out,
           s1, r1, s2, r2, s3, r3, s4, r4, s2e, r2e, s3e, r3e, spare, tensor, tensor_e, work, base,
           hx_send, hx, hy_send, hy, send, recv, hsend, hrecv):
    w, n = lax.axis_index("wide"), lax.axis_index("narrow")
    upper = jnp.where(w >= 32, 1, 0)
    mate = jnp.where(lax.rem(w, 32) == 0, 32 - w, WIDE - w)
    row_low = jnp.where(upper == 1, mate, w)
    row_high = jnp.where(upper == 1, w, mate)
    special = lax.rem(w, 32) == 0
    me = upper * NARROW + n

    def pair_device(t):
        return (jnp.where(t >= NARROW, row_high, row_low), lax.rem(t, NARROW))

    barrier = pltpu.get_barrier_semaphore()

    def greet_wide(i, carry):
        pl.semaphore_signal(barrier, inc=1, device_id=(lax.rem(w + i, WIDE), n), device_id_type=MESH)
        return carry

    def greet_pair(i, carry):
        pl.semaphore_signal(barrier, inc=1, device_id=pair_device(lax.rem(me + i, GROUP)), device_id_type=MESH)
        return carry

    lax.fori_loop(1, WIDE, greet_wide, 0)
    lax.fori_loop(1, GROUP, greet_pair, 0)

    direction = {}
    sat = {}
    for xx in range(2):
        rows = pl.ds(xx, NZ, stride=2)
        mag = region[rows, :].astype(F32)
        mat = material[rows, :]

        def lookup(table):
            out = jnp.full(mat.shape, table[3], F32)
            for i in range(3):
                out = jnp.where(mat == i, table[i], out)
            return out

        sat[xx] = lookup(satur)
        for c in range(3):
            direction[c, xx] = spin[c, rows, :] * mag
    moment = jnp.concatenate([direction[c, xx] * sat[xx] for xx in range(2) for c in range(3)], 1)
    spec = mm((zf_hi[...], zf_lo[...]), split(moment))
    re, im = spec[:WIDE], spec[WIDE:]
    left = low_half((32, MSG))
    s1[0:32, :] = jnp.where(left, re[:32], swap(im[:32]))
    s1[32:64, :] = jnp.where(left, swap(re[32:]), im[32:])

    lane = lax.broadcasted_iota(jnp.int32, (NZ, LANES), 1)
    for xx in range(2):
        for c in range(3):
            hx_send[1 - xx, NZ * c:NZ * c + NZ, :] = direction[c, xx]
        for side, at in ((0, LANES - 1), (1, 0)):
            cols = [jnp.broadcast_to(direction[c, xx][:, at:at + 1], (NZ, LANES)) for c in range(3)]
            hy_send[side, NZ * xx:NZ * xx + NZ, :] = jnp.where(
                lane == 0, cols[0], jnp.where(lane == 1, cols[1], cols[2]))

    pl.semaphore_wait(barrier, WIDE - 1 + GROUP - 1)

    def local(src, dst, sem):
        return pltpu.make_async_copy(src, dst, sem)

    def rows_start(src, dst, i, mine, count, device):
        def go(step, carry):
            t = lax.rem(mine + step, count)
            pltpu.make_async_remote_copy(
                src.at[pl.ds(t, 1)], dst.at[pl.ds(mine, 1)], send.at[i], recv.at[i],
                device_id=device(t), device_id_type=MESH).start()
            return carry
        lax.fori_loop(1, count, go, 0)
        own = src.at[pl.ds(mine, 1)]
        local(own, dst.at[pl.ds(mine, 1)], recv.at[i]).start()
        local(own, spare.at[pl.ds(0, 1), pl.ds(0, src.shape[1])], send.at[i]).start()

    def wide_device(t):
        return (t, n)

    def blocks_start(src, dst, i):
        def go(step, carry):
            t = lax.rem(me + step, GROUP)
            pltpu.make_async_remote_copy(
                src.at[t], dst.at[me], send.at[i], recv.at[i],
                device_id=pair_device(t), device_id_type=MESH).start()
            return carry
        lax.fori_loop(1, GROUP, go, 0)
        local(src.at[me], dst.at[me], recv.at[i]).start()

    def rows_wait(src, dst, i):
        local(dst, dst, recv.at[i]).wait()
        local(src, src, send.at[i]).wait()

    def blocks_wait(src, dst, i):
        local(dst, dst, recv.at[i]).wait()
        part = src.at[pl.ds(0, GROUP - 1)]
        local(part, part, send.at[i]).wait()

    halo = []
    for side, step in ((0, 1), (1, WIDE - 1)):
        halo.append(pltpu.make_async_remote_copy(
            hx_send.at[side], hx.at[side], hsend.at[side], hrecv.at[side],
            device_id=(lax.rem(w + step, WIDE), n), device_id_type=MESH))
    for side, step in ((0, 1), (1, NARROW - 1)):
        halo.append(pltpu.make_async_remote_copy(
            hy_send.at[side], hy.at[side], hsend.at[2 + side], hrecv.at[2 + side],
            device_id=(w, lax.rem(n + step, NARROW)), device_id_type=MESH))

    rows_start(s1, r1, 0, w, WIDE, wide_device)
    for copy in halo:
        copy.start()

    flat = demag_spec[...].reshape(6 * 32, LY)

    def reorder(q, carry):
        ky = lax.broadcasted_iota(jnp.int32, (LY, LANES), 0)
        col = lax.broadcasted_iota(jnp.int32, (LY, LANES), 1)
        target = 32 * (col & (HALF - 1)) + 2 * q + lax.shift_right_logical(col, 6)
        pick = jnp.where(ky == target, 1.0, 0.0).astype(BF16)
        got = jnp.dot(flat, pick, preferred_element_type=F32)
        other = pltpu.roll(got, HALF, 1)
        left = low_half(got.shape)
        for half, both in ((0, jnp.where(left, got, other)), (1, jnp.where(left, other, got))):
            at = pl.multiple_of(16 * q + 8 * half, 8)
            for g in range(6):
                for t in range(2):
                    tensor[t, g, pl.ds(at, 8), :] = both[32 * g + 8 * t:32 * g + 8 * t + 8]
            for d in range(3):
                extra = [both[32 * g + ROWS:32 * g + ROWS + 1] for g in DIAGONALS[d]]
                tensor_e[d, pl.ds(at, 8), :] = jnp.concatenate(extra + [jnp.zeros((5, LANES), F32)], 0)
        return carry

    lax.fori_loop(0, 16, reorder, 0)

    rows_wait(s1, r1, 0)
    got = r1[...]
    z = jnp.concatenate([got[:, :3 * LANES], got[:, 3 * LANES:]], 0)
    left = low_half(z.shape)
    sign = sign_of(z.shape)
    zero = jnp.zeros_like(z)
    z_swap = swap(z)
    low = jnp.where(special, jnp.where(left, z, zero), z)
    high = jnp.where(special, jnp.where(left, z_swap, zero), z * (-sign))
    rhs = jnp.concatenate([
        jnp.concatenate([low, high], 1),
        jnp.concatenate([swap(low) * sign, swap(high) * sign], 1)], 0)
    out = mm((xf_hi[...], xf_lo[...]), split(rhs))
    for q in range(2):
        part = out[:, 3 * LANES * q:3 * LANES * (q + 1)]
        for b in range(NARROW):
            s2[q * NARROW + b] = part[ROWS * b:ROWS * b + ROWS]
        s2e[q * NARROW:q * NARROW + NARROW, :] = part[NARROW * ROWS:]
    blocks_start(s2, r2, 1)
    rows_start(s2e, r2e, 2, me, GROUP, pair_device)

    for copy in halo:
        copy.wait()
    inside = [jnp.where(w > 0, 1.0, 0.0), jnp.where(w < WIDE - 1, 1.0, 0.0),
              jnp.where(n > 0, 1.0, 0.0), jnp.where(n < NARROW - 1, 1.0, 0.0)]
    for xx in range(2):
        total = [jnp.zeros((NZ, LANES), F32)] * 3
        weight = jnp.zeros((NZ, LANES), F32)
        here = [direction[c, xx] for c in range(3)]

        def x_halo(side):
            return [hx[side, NZ * c:NZ * c + NZ, :] * inside[side] for c in range(3)]

        def y_edge(side, c):
            column = hy[side, NZ * xx:NZ * xx + NZ, c:c + 1] * inside[2 + side]
            return jnp.broadcast_to(column, (NZ, LANES))

        neighbours = [
            [shifted(d, 1) for d in here],
            [shifted(d, -1) for d in here],
            [direction[c, 0] for c in range(3)] if xx == 1 else x_halo(0),
            [direction[c, 1] for c in range(3)] if xx == 0 else x_halo(1),
            [jnp.where(lane == LANES - 1, y_edge(1, c), pltpu.roll(here[c], LANES - 1, 1)) for c in range(3)],
            [jnp.where(lane == 0, y_edge(0, c), pltpu.roll(here[c], 1, 1)) for c in range(3)],
        ]
        for near in neighbours:
            total = [a + b for a, b in zip(total, near)]
            weight = weight + (near[0] * near[0] + near[1] * near[1] + near[2] * near[2])
        mat = material[pl.ds(xx, NZ, stride=2), :]
        anis_cell = jnp.full(mat.shape, aniso[3], F32)
        for i in range(3):
            anis_cell = jnp.where(mat == i, aniso[i], anis_cell)
        for c in range(3):
            part = EXCHANGE * (total[c] - weight * here[c]) / sat[xx] + applied[c]
            if c == 2:
                part = part + 2.0 * anis_cell / sat[xx] * here[2]
            base[c, NZ * xx:NZ * xx + NZ, :] = part

    blocks_wait(s2, r2, 1)
    rows_wait(s2e, r2e, 2)
    sign8 = sign_of((8, LANES))

    def source(b):
        return (b % 2) * NARROW + b // 2

    def y_forward(v):
        even = fft(v, -1, sign8)
        odd = fft([turn(x, -2 * math.pi * b / 32, sign8) for b, x in enumerate(v)], -1, sign8)
        for k in range(32):
            u = even[k // 2] if k % 2 == 0 else odd[k // 2]
            work[8 * k:8 * k + 8, :] = (
                u * twist[0, k:k + 1, :] + pltpu.roll(u, HALF, 1) * twist[1, k:k + 1, :])
        return mm(split(work[...]), (wf_hi[...], wf_lo[...]))

    def y_inverse(field):
        work[...] = mm(split(field), (wi_hi[...], wi_lo[...]))
        u = []
        for k in range(32):
            x = work[8 * k:8 * k + 8, :]
            u.append(x * twist[0, k:k + 1, :] - pltpu.roll(x, HALF, 1) * twist[1, k:k + 1, :])
        even = fft(u[0::2], 1, sign8)
        odd = fft(u[1::2], 1, sign8)
        return [even[b] + turn(odd[b], 2 * math.pi * b / 32, sign8) for b in range(16)]

    def y_block(t, carry):
        rows = pl.ds(pl.multiple_of(8 * t, 8), 8)
        spectra = [
            y_forward([r2[source(b), rows, LANES * c:LANES * c + LANES] for b in range(16)])
            for c in range(3)
        ]
        for c, picks in enumerate(ROWS_OF):
            field = -(tensor[t, picks[0]] * spectra[0] + tensor[t, picks[1]] * spectra[1]
                      + tensor[t, picks[2]] * spectra[2])
            for b, x in enumerate(y_inverse(field)):
                s3[source(b), rows, LANES * c:LANES * c + LANES] = x
        return carry

    lax.fori_loop(0, 2, y_block, 0)
    blocks_start(s3, r3, 3)
    v = []
    for b in range(16):
        row = [r2e[source(b):source(b) + 1, LANES * c:LANES * c + LANES] for c in range(3)]
        v.append(jnp.concatenate(row + row + row[:2], 0))
    spectrum = y_forward(v)
    field = -(tensor_e[0] * spectrum + tensor_e[1] * pltpu.roll(spectrum, 255, 0)
              + tensor_e[2] * pltpu.roll(spectrum, 254, 0))
    for b, x in enumerate(y_inverse(field)):
        for c in range(3):
            s3e[source(b):source(b) + 1, LANES * c:LANES * c + LANES] = x[c:c + 1]
    rows_start(s3e, r3e, 4, me, GROUP, pair_device)
    blocks_wait(s3, r3, 3)
    rows_wait(s3e, r3e, 4)

    got = r3[...].reshape(GROUP * ROWS, 3 * LANES)
    low = jnp.concatenate([got[:NARROW * ROWS], r3e[:NARROW, :]], 0)
    high = jnp.concatenate([got[NARROW * ROWS:], r3e[NARROW:, :]], 0)
    sign = sign_of(low.shape)
    rhs = jnp.concatenate([
        jnp.concatenate([low, high], 1),
        jnp.concatenate([swap(low) * sign, swap(high) * sign], 1)], 0)
    out = mm((xi_hi[...], xi_lo[...]), split(rhs))
    low, high = out[:, :3 * LANES], out[:, 3 * LANES:]
    left = low_half(low.shape)
    sign = sign_of(low.shape)
    slot = jnp.where(special, jnp.where(left, low, swap(high)), low - high * sign)
    s4[:, :3 * LANES] = slot[:WIDE]
    s4[:, 3 * LANES:] = slot[WIDE:]
    rows_start(s4, r4, 5, w, WIDE, wide_device)
    rows_wait(s4, r4, 5)

    got = r4[...]
    first, second = got[:32], got[32:]
    left = low_half(first.shape)
    zero = jnp.zeros_like(first)
    rhs = jnp.concatenate([
        jnp.where(left, first, zero), jnp.where(left, swap(first), zero),
        jnp.where(left, zero, swap(second)), jnp.where(left, zero, second)], 0)
    field = mm((zi_hi[...], zi_lo[...]), split(rhs))
    for xx in range(2):
        rows = pl.ds(xx, NZ, stride=2)
        h = []
        for c in range(3):
            at = LANES * (3 * xx + c)
            h.append(field[:, at:at + LANES])
            demag_out[c, rows, :] = h[c]
        mat = material[rows, :]
        a = jnp.full(mat.shape, damp[3], F32)
        for i in range(3):
            a = jnp.where(mat == i, damp[i], a)
        h = [h[c] + base[c, NZ * xx:NZ * xx + NZ, :] for c in range(3)]
        d = [direction[c, xx] for c in range(3)]

        def cross(x, y):
            return [x[1] * y[2] - x[2] * y[1], x[2] * y[0] - x[0] * y[2], x[0] * y[1] - x[1] * y[0]]

        torque = cross(d, h)
        second_torque = cross(d, torque)
        for c in range(3):
            rate_out[c, rows, :] = -(torque[c] + a * second_torque[c]) / (1.0 + a * a)


def shards(spin, region, material, saturation, anisotropy, damping, applied, demag_spectrum):
    vmem = pl.BlockSpec(memory_space=pltpu.VMEM)
    smem = pl.BlockSpec(memory_space=pltpu.SMEM)
    tables = []
    for table in (z_forward(), z_inverse(), x_forward(), x_inverse(), y_inner(-1), y_inner(1)):
        tables.extend(jnp.asarray(part) for part in halves(table))
    tables.append(jnp.asarray(y_twist()))
    dma = pltpu.SemaphoreType.DMA
    out = jax.ShapeDtypeStruct((3, 2 * NZ, LANES), F32)
    rate, demag = pl.pallas_call(
        kernel,
        out_shape=(out, out),
        in_specs=[vmem] * 3 + [smem] * 4 + [vmem] * (1 + len(tables)),
        out_specs=(vmem, vmem),
        scratch_shapes=[pltpu.VMEM((WIDE, MSG), F32)] * 2
        + [pltpu.VMEM((GROUP, ROWS, 3 * LANES), F32)] * 4
        + [pltpu.VMEM((WIDE, MSG), F32)] * 2
        + [pltpu.VMEM((GROUP, 3 * LANES), F32)] * 4
        + [
            pltpu.VMEM((8, MSG), F32),
            pltpu.VMEM((2, 6, 256, LANES), F32),
            pltpu.VMEM((3, 256, LANES), F32),
            pltpu.VMEM((256, LANES), F32),
            pltpu.VMEM((3, 2 * NZ, LANES), F32),
            pltpu.VMEM((2, 3 * NZ, LANES), F32),
            pltpu.VMEM((2, 3 * NZ, LANES), F32),
            pltpu.VMEM((2, 2 * NZ, LANES), F32),
            pltpu.VMEM((2, 2 * NZ, LANES), F32),
        ]
        + [dma((6,)), dma((6,)), dma((4,)), dma((4,))],
        compiler_params=pltpu.CompilerParams(
            collective_id=0, has_side_effects=True, vmem_limit_bytes=40 * 2**20
        ),
    )(
        spin.reshape(3, 2 * NZ, LANES), region.reshape(2 * NZ, LANES), material.reshape(2 * NZ, LANES),
        saturation, anisotropy, damping, applied, demag_spectrum.reshape(6, 32, LY), *tables,
    )
    return rate.reshape(3, NZ, 2, LANES), demag.reshape(3, NZ, 2, LANES)


def solution(mesh):
    placed = (
        P(None, None, "wide", "narrow"),
        P(None, "wide", "narrow"),
        P(None, "wide", "narrow"),
        P(),
        P(),
        P(),
        P(),
        P(None, "wide", "narrow", None),
    )
    return jax.shard_map(
        shards,
        mesh=mesh,
        in_specs=placed,
        out_specs=(P(None, None, "wide", "narrow"), P(None, None, "wide", "narrow")),
        check_vma=False,
    )
```

profile of v0, /device:TPU:1, one launch (start us, length us, event | category | flops | bytes accessed | tf_op | source)
XLA Modules:
  0.0 113.7 jit_solution(10624121536614824228)
XLA Ops:
  0.6 0.0 copy-start.15
  0.6 0.0 copy-start.20
  0.7 0.0 copy-start.17
  0.7 0.0 copy-start.18
  0.7 0.0 copy-start.19
  0.7 0.6 copy-done.15
  1.3 0.0 copy-done.20
  1.3 0.0 copy-done.17
  1.3 0.0 copy-done.18
  1.3 0.0 copy-done.19
  1.4 0.0 copy-start
  1.4 1.1 copy-done
  2.5 0.0 copy-start.1
  2.5 0.9 copy-done.1
  3.4 0.0 copy-start.2
  3.4 0.9 copy-done.2
  4.3 0.9 copy-done.3
  5.2 0.9 copy-done.4
  6.1 0.9 copy-done.5
  6.9 0.8 copy-done.6
  7.7 0.8 copy-done.7
  8.5 0.8 copy-done.8
  9.2 0.8 copy-done.9
  10.0 0.8 copy-done.10
  10.7 0.8 copy-done.11
  11.5 0.8 copy-done.12
  12.2 0.8 copy-done.13
  13.0 0.8 copy-done.14
  13.8 0.7 copy-done.16
  14.5 98.0 %shard_map.212 = (f32[3,64,128]{2,1,0:T(8,128)S(1)}, f32[3,64,128]{2,1,0:T(8,128)S(1)}) custom-call(f32[3,64,128]{2,1,0:T(8,128)S(1)} %bitcast.7, s32[64,128]{1,0:T(8,128)S(1)} %bitcast.10, s32[64,128]{1,0:T(8,128)S(1)} %bitcast.11, f32[4]{0:T(128)S(1)} %copy-done.17, f32[4]{0:T(128)S(1)} %copy-done.18, f32[4]{0:T(128)S(1)} %copy-done.19, f32[3]{0:T(128)S(1)} %copy-done.20, ...), custom_call_target="tpu_custom_call" | custom-call | tf_op jit(solution)/shard_map/pallas_call | solution.py:454
  112.4 0.6 copy.25
  113.1 0.6 copy.26
  (13 shorter events, 0.0 us)
Async XLA Ops:
  0.6 0.7 copy-start.15
  0.6 0.7 copy-start.20
  0.7 0.7 copy-start.17
  0.7 0.7 copy-start.18
  0.7 0.7 copy-start.19
  1.4 1.1 copy-start
  2.5 0.9 copy-start.1
  3.4 0.9 copy-start.2
  4.3 0.9 copy-start.3
  5.2 0.9 copy-start.4
  6.1 0.9 copy-start.5
  6.9 0.8 copy-start.6
  7.7 0.8 copy-start.7
  8.5 0.8 copy-start.8
  9.2 0.8 copy-start.9
  10.0 0.8 copy-start.10
  10.7 0.8 copy-start.11
  11.5 0.8 copy-start.12
  12.2 0.8 copy-start.13
  13.0 0.8 copy-start.14
  13.8 0.7 copy-start.16
where the time goes:
time: 115 us; the launch traced here: 114 us
  Pallas kernels  98 us (85%)
  local copies, waits for them, and re-layouts  15 us (13%)
    pallas_call x1, Pallas kernels, shards(): pl.pallas_call(kernel, out_shape=(out, out), in_specs=[vmem] * 3 + [smem]...  98 us
    unnamed x44, local copies, waits for them, and re-layouts  15 us

commit v1 on v0

v1 whole, which is shorter than its diff:
```python
import functools
import math

import jax
import jax.numpy as jnp
import ml_dtypes
import numpy as np
from jax import lax
from jax.experimental import pallas as pl
from jax.experimental.pallas import tpu as pltpu
from jax.sharding import PartitionSpec as P

EXCHANGE = 0.3
MESH = pl.DeviceIdType.MESH
WIDE, NARROW = 64, 8
NZ, LZ, NX, LX, NY, LY = 32, 64, 128, 256, 1024, 2048
SLOTS = 32
ROWS = 32
K = 16
LANES = 128
F32, BF16 = jnp.float32, jnp.bfloat16
ROWS_OF = ((0, 3, 4), (3, 1, 5), (4, 5, 2))


def halves(x):
    hi = x.astype(np.float32).astype(ml_dtypes.bfloat16)
    lo = (x - hi.astype(np.float64)).astype(ml_dtypes.bfloat16)
    return np.stack([hi, lo])


def z_parts():
    s, z = np.arange(SLOTS)[:, None], np.arange(NZ)[None]
    angle = 2 * np.pi * (s * z % LZ) / LZ
    re = np.cos(angle)
    im = np.where(s == 0, np.where(z % 2, -1.0, 1.0), -np.sin(angle))
    return re, im


def z_forward():
    return np.concatenate(z_parts(), 0)


def z_inverse():
    re, im = z_parts()
    return np.concatenate([re, re, im, im], 0).T


def complex_matrix(angle):
    c, s = np.cos(angle), np.sin(angle)
    return np.block([[c, -s], [s, c]])


def x_angle():
    x = np.arange(NX).reshape(WIDE, 2).T.reshape(-1)
    return 2 * np.pi * (np.arange(NX)[:, None] * x[None] % LX) / LX


def y_angle():
    p = np.arange(LANES)
    return 2 * np.pi * (p[:, None] * p[None] % LANES) / LANES


def square_tables():
    angle = x_angle()
    tables = [
        complex_matrix(-angle),
        complex_matrix(angle.T) * (2.0 / (LZ * LX * LY)),
        complex_matrix(-y_angle()).T,
        complex_matrix(y_angle()).T,
    ]
    return np.stack([halves(t) for t in tables])


def y_twist():
    k, p = np.arange(K)[:, None], np.arange(LANES)[None]
    angle = 2 * np.pi * (k * p) / LY
    return np.stack([np.cos(angle), -np.sin(angle)]).astype(np.float32)


def mm(a, b):
    dot = functools.partial(jnp.dot, preferred_element_type=F32)
    return dot(a[0], b[0]) + (dot(a[0], b[1]) + dot(a[1], b[0]))


def split(x):
    hi = x.astype(BF16)
    return hi, (x - hi.astype(F32)).astype(BF16)


def turn(v, angle):
    c, s = math.cos(angle), math.sin(angle)
    re, im = v
    if abs(s) < 1e-9 and c > 0:
        return v
    if abs(c) < 1e-9:
        return (-im, re) if s > 0 else (im, -re)
    if abs(c - s) < 1e-9:
        return ((re - im) * c, (re + im) * c)
    if abs(c + s) < 1e-9:
        return ((re + im) * c, (im - re) * c)
    return (re * c - im * s, re * s + im * c)


def fft(values, direction):
    n = len(values)
    if n == 1:
        return values
    even = fft(values[0::2], direction)
    odd = fft(values[1::2], direction)
    odd = [turn(o, direction * 2 * math.pi * k / n) for k, o in enumerate(odd)]
    return ([(e[0] + o[0], e[1] + o[1]) for e, o in zip(even, odd)]
            + [(e[0] - o[0], e[1] - o[1]) for e, o in zip(even, odd)])


def shifted(x, step):
    zero = jnp.zeros((1, x.shape[1]), x.dtype)
    if step > 0:
        return jnp.concatenate([x[1:], zero], 0)
    return jnp.concatenate([zero, x[:-1]], 0)


def cross(x, y):
    return [x[1] * y[2] - x[2] * y[1], x[2] * y[0] - x[0] * y[2], x[0] * y[1] - x[1] * y[0]]


def pick(mat, table):
    out = jnp.full(mat.shape, table[3], F32)
    for i in range(3):
        out = jnp.where(mat == i, table[i], out)
    return out


def other_bit(bit, slot):
    return lax.rem(bit + slot, 2)


def kernel(spin_hbm, region_hbm, material_hbm, satur, aniso, damp, applied, spec_hbm,
           zf_hbm, zi_hbm, square_hbm, twist_hbm,
           rate_out, demag_out,
           spin, region, material, spec, zf, zi, square, twist,
           s1, r1, s2, r2, s3, r3, s4, r4, tensor, work, spectra, direction, satcell, base,
           hx_send, hx, hy_send, hy, spare_row, spare,
           load, send1, recv1, send2, recv2, send3, recv3, send4, recv4, hsend, hrecv):
    w, n = lax.axis_index("wide"), lax.axis_index("narrow")
    half, column = n // 4, lax.rem(n, 4)
    slot = lax.rem(w, SLOTS)
    part = other_bit(w // SLOTS, slot)
    special = slot == 0
    y_device = w <= SLOTS

    loads = [pltpu.make_async_copy(a, b, load.at[i]) for i, (a, b) in enumerate((
        (spin_hbm, spin), (region_hbm, region), (material_hbm, material), (zf_hbm, zf),
        (spec_hbm, spec), (square_hbm, square), (twist_hbm, twist), (zi_hbm, zi)))]
    for copy in loads:
        copy.start()

    def spectrum_device(i):
        return (lax.rem(i, SLOTS) + SLOTS * other_bit(half, i), 4 * (i // SLOTS) + column)

    def brick_device(i):
        return (i, 4 * part + column)

    def is_me(device):
        return (device[0] == w) & (device[1] == n)

    def line_device(i):
        return (jnp.where(i >= 4, SLOTS, slot), 4 * half + lax.rem(i, 4))

    def plane_device(i):
        return (slot + SLOTS * other_bit(i // 4, slot), 4 * half + lax.rem(i, 4))

    barrier = pltpu.get_barrier_semaphore()

    def greet(device):
        @pl.when(jnp.logical_not(is_me(device)))
        def _():
            pl.semaphore_signal(barrier, inc=1, device_id=device, device_id_type=MESH)

    def greet_all(count, device):
        def go(i, carry):
            greet(device(i))
            return carry
        lax.fori_loop(0, count, go, 0)

    greet_all(64, spectrum_device)
    greet_all(64, brick_device)
    greet_all(jnp.where(special, 8, 4), line_device)

    @pl.when(y_device)
    def _():
        greet_all(8, plane_device)

    sides = [(lax.rem(w + 1, WIDE), n), (lax.rem(w + WIDE - 1, WIDE), n),
             (w, lax.rem(n + 1, NARROW)), (w, lax.rem(n + NARROW - 1, NARROW))]
    for device in sides:
        greet(device)
    on_both = half == part
    expected = (128 - 2 * jnp.where(on_both, 1, 0)
                + jnp.where(special, 8, 4) - jnp.where(w <= SLOTS, 1, 0)
                + jnp.where(y_device, 7, 0) + 4)

    for copy in loads[:4]:
        copy.wait()
    for xx in range(2):
        rows = pl.ds(xx, NZ, stride=2)
        mag = region[rows, :].astype(F32)
        satcell[xx] = pick(material[rows, :], satur)
        for c in range(3):
            direction[c, xx] = spin[c, rows, :] * mag
    for c in range(3):
        moment = jnp.concatenate([direction[c, xx] * satcell[xx] for xx in range(2)], 1)
        out = mm((zf[0], zf[1]), split(moment))
        s1[:, 512 * c:512 * c + 256] = out[:SLOTS]
        s1[:, 512 * c + 256:512 * c + 512] = out[SLOTS:]

    lane = lax.broadcasted_iota(jnp.int32, (NZ, LANES), 1)
    for xx in range(2):
        for c in range(3):
            hx_send[1 - xx, NZ * c:NZ * c + NZ, :] = direction[c, xx]
        for side, at in ((0, LANES - 1), (1, 0)):
            cols = [jnp.broadcast_to(direction[c, xx][:, at:at + 1], (NZ, LANES)) for c in range(3)]
            hy_send[side, NZ * xx:NZ * xx + NZ, :] = jnp.where(
                lane == 0, cols[0], jnp.where(lane == 1, cols[1], cols[2]))

    pl.semaphore_wait(barrier, expected)

    def local(src, dst, sem):
        return pltpu.make_async_copy(src, dst, sem)

    def put(src, dst, dump, send, recv, device):
        @pl.when(is_me(device))
        def _():
            local(src, dst, recv).start()
            local(src, dump, send).start()

        @pl.when(jnp.logical_not(is_me(device)))
        def _():
            pltpu.make_async_remote_copy(
                src, dst, send, recv, device_id=device, device_id_type=MESH).start()

    def done(ref, sem):
        local(ref, ref, sem).wait()


    def spectra_start():
        def go(step, carry):
            i = lax.rem(w + step, 64)
            put(s1.at[pl.ds(lax.rem(i, SLOTS), 1)], r1.at[pl.ds(w, 1)], spare_row.at[pl.ds(0, 1)],
                send1, recv1, spectrum_device(i))
            return carry
        lax.fori_loop(0, 64, go, 0)

    def bricks_start():
        def go(step, carry):
            i = lax.rem(w + step, 64)
            put(s4.at[pl.ds(i, 1)], r4.at[pl.ds(SLOTS * half + slot, 1)], spare_row.at[pl.ds(8, 1)],
                send4, recv4, brick_device(i))
            return carry
        lax.fori_loop(0, 64, go, 0)

    def lines_start(c):
        def go(i, carry):
            put(s2.at[c, i], r2.at[c, 4 * part + column], spare.at[c], send2.at[c], recv2.at[c], line_device(i))
            return carry
        lax.fori_loop(0, jnp.where(special, 8, 4), go, 0)

    def planes_start(c):
        def go(i, carry):
            put(s3.at[c, i], r3.at[c, column + jnp.where(w == SLOTS, 4, 0)], spare.at[3 + c],
                send3.at[c], recv3.at[c], plane_device(i))
            return carry
        lax.fori_loop(0, 8, go, 0)

    def done_blocks(ref, sem):
        @pl.when(special)
        def _():
            done(ref, sem)

        @pl.when(jnp.logical_not(special))
        def _():
            done(ref.at[pl.ds(0, 4)], sem)

    halo = [pltpu.make_async_remote_copy(
        src, dst, hsend.at[i], hrecv.at[i], device_id=sides[i], device_id_type=MESH)
        for i, (src, dst) in enumerate((
            (hx_send.at[0], hx.at[0]), (hx_send.at[1], hx.at[1]),
            (hy_send.at[0], hy.at[0]), (hy_send.at[1], hy.at[1])))]

    spectra_start()
    for copy in halo:
        copy.start()
    for copy in loads[4:]:
        copy.wait()

    @pl.when(y_device)
    def _():
        flat = spec[...].reshape(6 * ROWS, LY)

        def reorder(k, carry):
            ky = lax.broadcasted_iota(jnp.int32, (LY, LANES), 0)
            col = lax.broadcasted_iota(jnp.int32, (LY, LANES), 1)
            choose = jnp.where(ky == K * col + k, 1.0, 0.0).astype(BF16)
            got = jnp.dot(flat, choose, preferred_element_type=F32)
            for g in range(6):
                for t in range(4):
                    tensor[g, pl.ds(pl.multiple_of(128 * t + 8 * k, 8), 8), :] = (
                        got[ROWS * g + 8 * t:ROWS * g + 8 * t + 8])
            return carry

        lax.fori_loop(0, K, reorder, 0)

    flip = jnp.where(half == 1, -1.0, 1.0).astype(F32)

    def x_forward(c):
        got = r1[:, 512 * c:512 * c + 512]
        re = jnp.concatenate([got[:, 0:128], got[:, 128:256] * flip], 0)
        im = jnp.concatenate([got[:, 256:384], got[:, 384:512] * flip], 0)
        rhs = jnp.concatenate([re, jnp.where(special, jnp.zeros_like(im), im)], 0)

        def store(out, at):
            for i in range(4):
                s2[c, at + i, :, 0:128] = out[ROWS * i:ROWS * i + ROWS]
                s2[c, at + i, :, 128:256] = out[128 + ROWS * i:128 + ROWS * i + ROWS]

        store(mm((square[0, 0], square[0, 1]), split(rhs)), 0)

        @pl.when(special)
        def _():
            other = jnp.concatenate([im, jnp.zeros_like(im)], 0)
            store(mm((square[0, 0], square[0, 1]), split(other)), 4)

        lines_start(c)

    done(r1, recv1)
    for c in range(3):
        x_forward(c)

    def y_forward(c):
        done(r2.at[c], recv2.at[c])

        def go(t, carry):
            rows = pl.ds(pl.multiple_of(8 * t, 8), 8)
            v = [(r2[c, b, rows, 0:128], r2[c, b, rows, 128:256]) for b in range(8)]
            even = fft(v, -1)
            odd = fft([turn(x, -2 * math.pi * b / K) for b, x in enumerate(v)], -1)
            for k in range(K):
                re, im = even[k // 2] if k % 2 == 0 else odd[k // 2]
                cos, sin = twist[0, k:k + 1, :], twist[1, k:k + 1, :]
                at = pl.ds(pl.multiple_of(128 * t + 8 * k, 8), 8)
                work[at, 0:128] = re * cos - im * sin
                work[at, 128:256] = re * sin + im * cos
            return carry

        lax.fori_loop(0, 4, go, 0)

        def multiply(t, carry):
            rows = pl.ds(pl.multiple_of(256 * t, 256), 256)
            spectra[c, rows, :] = mm(split(work[rows, :]), (square[2, 0], square[2, 1]))
            return carry

        lax.fori_loop(0, 2, multiply, 0)

    def y_inverse(c):
        a, b, d = ROWS_OF[c]

        def multiply(t, carry):
            rows = pl.ds(pl.multiple_of(256 * t, 256), 256)
            field = [-(tensor[a, rows, :] * spectra[0, rows, at:at + 128]
                       + tensor[b, rows, :] * spectra[1, rows, at:at + 128]
                       + tensor[d, rows, :] * spectra[2, rows, at:at + 128]) for at in (0, 128)]
            work[rows, :] = mm(split(jnp.concatenate(field, 1)), (square[3, 0], square[3, 1]))
            return carry

        lax.fori_loop(0, 2, multiply, 0)

        def go(t, carry):
            u = []
            for k in range(K):
                at = pl.ds(pl.multiple_of(128 * t + 8 * k, 8), 8)
                re, im = work[at, 0:128], work[at, 128:256]
                cos, sin = twist[0, k:k + 1, :], twist[1, k:k + 1, :]
                u.append((re * cos + im * sin, im * cos - re * sin))
            even = fft(u[0::2], 1)
            odd = fft(u[1::2], 1)
            rows = pl.ds(pl.multiple_of(8 * t, 8), 8)
            for j in range(8):
                o = turn(odd[j], 2 * math.pi * j / K)
                s3[c, j, rows, 0:128] = even[j][0] + o[0]
                s3[c, j, rows, 128:256] = even[j][1] + o[1]
            return carry

        lax.fori_loop(0, 4, go, 0)
        planes_start(c)

    def x_inverse(c):
        done_blocks(r3.at[c], recv3.at[c])

        def transform(at):
            got = r3[c, at:at + 4].reshape(4 * ROWS, 256)
            rhs = jnp.concatenate([got[:, 0:128], got[:, 128:256]], 0)
            return mm((square[1, 0], square[1, 1]), split(rhs))

        def store(out, at):
            at += 512 * c
            s4[:, at:at + 128] = out[:WIDE]
            s4[:, at + 128:at + 256] = out[WIDE:] * flip

        out = transform(0) * jnp.where(special, 0.5, 1.0).astype(F32)
        store(out[:NX], 0)

        @pl.when(jnp.logical_not(special))
        def _():
            store(out[NX:], 256)

        @pl.when(special)
        def _():
            store(transform(4)[:NX] * 0.5, 256)

    @pl.when(y_device)
    def _():
        for c in range(3):
            y_forward(c)
        y_inverse(0)
        y_inverse(1)

    x_inverse(0)

    @pl.when(y_device)
    def _():
        y_inverse(2)

    x_inverse(1)
    x_inverse(2)
    bricks_start()

    for copy in halo:
        copy.wait()
    inside = [jnp.where(w > 0, 1.0, 0.0), jnp.where(w < WIDE - 1, 1.0, 0.0),
              jnp.where(n > 0, 1.0, 0.0), jnp.where(n < NARROW - 1, 1.0, 0.0)]
    for xx in range(2):
        total = [jnp.zeros((NZ, LANES), F32)] * 3
        weight = jnp.zeros((NZ, LANES), F32)
        here = [direction[c, xx] for c in range(3)]
        sat = satcell[xx]

        def x_halo(side):
            return [hx[side, NZ * c:NZ * c + NZ, :] * inside[side] for c in range(3)]

        def y_edge(side, c):
            edge = hy[side, NZ * xx:NZ * xx + NZ, c:c + 1] * inside[2 + side]
            return jnp.broadcast_to(edge, (NZ, LANES))

        neighbours = [
            [shifted(d, 1) for d in here],
            [shifted(d, -1) for d in here],
            [direction[c, 0] for c in range(3)] if xx == 1 else x_halo(0),
            [direction[c, 1] for c in range(3)] if xx == 0 else x_halo(1),
            [jnp.where(lane == LANES - 1, y_edge(1, c), pltpu.roll(here[c], LANES - 1, 1)) for c in range(3)],
            [jnp.where(lane == 0, y_edge(0, c), pltpu.roll(here[c], 1, 1)) for c in range(3)],
        ]
        for near in neighbours:
            total = [a + b for a, b in zip(total, near)]
            weight = weight + (near[0] * near[0] + near[1] * near[1] + near[2] * near[2])
        anis = pick(material[pl.ds(xx, NZ, stride=2), :], aniso)
        for c in range(3):
            field = EXCHANGE * (total[c] - weight * here[c]) / sat + applied[c]
            if c == 2:
                field = field + 2.0 * anis / sat * here[2]
            base[c, xx] = field

    done(r4, recv4)
    for c in range(3):
        got = r4[:, 512 * c:512 * c + 512]
        rhs = jnp.concatenate([got[:, 0:256], got[:, 256:512]], 0)
        out = mm((zi[0], zi[1]), split(rhs))
        for xx in range(2):
            h = out[:, LANES * xx:LANES * xx + LANES]
            demag_out[c, pl.ds(xx, NZ, stride=2), :] = h
            base[c, xx] = base[c, xx] + h
    for xx in range(2):
        rows = pl.ds(xx, NZ, stride=2)
        a = pick(material[rows, :], damp)
        d = [direction[c, xx] for c in range(3)]
        torque = cross(d, [base[c, xx] for c in range(3)])
        second = cross(d, torque)
        for c in range(3):
            rate_out[c, rows, :] = -(torque[c] + a * second[c]) / (1.0 + a * a)

    done(r1, send1)
    done(s4, send4)
    for c in range(3):
        done_blocks(s2.at[c], send2.at[c])

    @pl.when(y_device)
    def _():
        for c in range(3):
            done(s3.at[c], send3.at[c])


def shards(spin, region, material, saturation, anisotropy, damping, applied, demag_spectrum):
    vmem = pl.BlockSpec(memory_space=pltpu.VMEM)
    smem = pl.BlockSpec(memory_space=pltpu.SMEM)
    hbm = pl.BlockSpec(memory_space=pltpu.HBM)
    tables = [jnp.asarray(t) for t in (halves(z_forward()), halves(z_inverse()), square_tables(), y_twist())]
    dma = pltpu.SemaphoreType.DMA
    out = jax.ShapeDtypeStruct((3, 2 * NZ, LANES), F32)
    big = [spin.reshape(3, 2 * NZ, LANES), region.reshape(2 * NZ, LANES), material.reshape(2 * NZ, LANES)]
    spec = demag_spectrum.reshape(6, ROWS, LY)

    def room(x):
        return pltpu.VMEM(x.shape, x.dtype)

    rate, demag = pl.pallas_call(
        kernel,
        out_shape=(out, out),
        in_specs=[hbm] * 3 + [smem] * 4 + [hbm] * (1 + len(tables)),
        out_specs=(vmem, vmem),
        scratch_shapes=[room(x) for x in big + [spec] + tables]
        + [
            pltpu.VMEM((SLOTS, 1536), F32),
            pltpu.VMEM((64, 1536), F32),
        ]
        + [pltpu.VMEM((3, 8, ROWS, 256), F32)] * 4
        + [pltpu.VMEM((64, 1536), F32)] * 2
        + [
            pltpu.VMEM((6, 512, LANES), F32),
            pltpu.VMEM((512, 256), F32),
            pltpu.VMEM((3, 512, 256), F32),
            pltpu.VMEM((3, 2, NZ, LANES), F32),
            pltpu.VMEM((2, NZ, LANES), F32),
            pltpu.VMEM((3, 2, NZ, LANES), F32),
            pltpu.VMEM((2, 3 * NZ, LANES), F32),
            pltpu.VMEM((2, 3 * NZ, LANES), F32),
            pltpu.VMEM((2, 2 * NZ, LANES), F32),
            pltpu.VMEM((2, 2 * NZ, LANES), F32),
            pltpu.VMEM((16, 1536), F32),
            pltpu.VMEM((6, ROWS, 256), F32),
        ]
        + [dma((8,))]
        + [dma] * 2 + [dma((3,))] * 4 + [dma] * 2
        + [dma((4,)), dma((4,))],
        compiler_params=pltpu.CompilerParams(
            collective_id=0, has_side_effects=True, vmem_limit_bytes=56 * 2**20
        ),
    )(*big, saturation, anisotropy, damping, applied, spec, *tables)
    return rate.reshape(3, NZ, 2, LANES), demag.reshape(3, NZ, 2, LANES)


def solution(mesh):
    placed = (
        P(None, None, "wide", "narrow"),
        P(None, "wide", "narrow"),
        P(None, "wide", "narrow"),
        P(),
        P(),
        P(),
        P(),
        P(None, "wide", "narrow", None),
    )
    return jax.shard_map(
        shards,
        mesh=mesh,
        in_specs=placed,
        out_specs=(P(None, None, "wide", "narrow"), P(None, None, "wide", "narrow")),
        check_vma=False,
    )
```

time: 115 us -> 88.5 us (0.77)
  the two profiles are of different devices: /device:TPU:1 before, /device:TPU:57 now
where the time goes in v1:
time: 88.5 us; the launch traced here: 88.3 us
  Pallas kernels  85.4 us (96%)
  local copies, waits for them, and re-layouts  2.22 us (3%)
    pallas_call x1, Pallas kernels, shards(): pl.pallas_call(kernel, out_shape=(out, out), in_specs=[hbm] * 3 + [smem]...  85.4 us
    unnamed x4, local copies, waits for them, and re-layouts  2.22 us

profile of v1, /device:TPU:57, one launch (start us, length us, event | category | flops | bytes accessed | tf_op | source)
XLA Modules:
  0.0 88.3 jit_solution(10574778858685674746)
XLA Ops:
  0.6 85.4 %shard_map.131 = (f32[3,64,128]{2,1,0:T(8,128)}, f32[3,64,128]{2,1,0:T(8,128)}) custom-call(f32[3,64,128]{2,1,0:T(8,128)} %bitcast.7, s32[64,128]{1,0:T(8,128)} %bitcast.10, s32[64,128]{1,0:T(8,128)} %bitcast.11, f32[4]{0:T(128)} %satur.1, f32[4]{0:T(128)} %aniso.1, f32[4]{0:T(128)} %damp.1, f32[3]{0:T(128)} %applied.1, bf16[6,32,2048]{2,1,0:T(8,128)(2,1)} %bitcast.6, ...), custom_call_target="tpu_custom_call" | custom-call | tf_op jit(solution)/shard_map/pallas_call | solution.py:513
  86.1 0.0 copy-start
  86.1 1.6 %copy.16 = f32[3,32,2,128]{3,2,1,0:T(2,128)} copy(f32[3,32,2,128]{3,2,1,0:T(2,128)} %bitcast.9) | data formatting | bytes 196608
  87.6 0.0 copy-done
  87.7 0.6 copy.17
Async XLA Ops:
  86.1 1.6 %copy-start = (f32[3,64,128]{2,1,0:T(8,128)S(1)}, f32[3,64,128]{2,1,0:T(8,128)}, u32[]{:S(2)}) copy-start(f32[3,64,128]{2,1,0:T(8,128)} %get-tuple-element.5) | copy-start | bytes 294916

commit v2 on v1

--- a/solution.py
+++ b/solution.py
@@ -18,6 +18,9 @@
 ROWS = 32
 K = 16
 LANES = 128
+UNROLL = 9
+S1_CHUNKS = ((0, 1), (2,))
+S4_CHUNKS = ((0,), (1, 2))
 F32, BF16 = jnp.float32, jnp.bfloat16
 ROWS_OF = ((0, 3, 4), (3, 1, 5), (4, 5, 2))
 
@@ -171,10 +174,13 @@
 
     barrier = pltpu.get_barrier_semaphore()
 
+    def signal(device):
+        pl.semaphore_signal(barrier, inc=1, device_id=device, device_id_type=MESH)
+
     def greet(device):
         @pl.when(jnp.logical_not(is_me(device)))
         def _():
-            pl.semaphore_signal(barrier, inc=1, device_id=device, device_id_type=MESH)
+            signal(device)
 
     def greet_all(count, device):
         def go(i, carry):
@@ -182,8 +188,21 @@
             return carry
         lax.fori_loop(0, count, go, 0)
 
-    greet_all(64, spectrum_device)
-    greet_all(64, brick_device)
+    on_both = half == part
+
+    def greet_brick(i, carry):
+        signal(brick_device(lax.rem(w + i, WIDE)))
+        return carry
+
+    @pl.when(jnp.logical_not(on_both))
+    def _():
+        signal(brick_device(w))
+    lax.fori_loop(1, WIDE, greet_brick, 0, unroll=UNROLL)
+
+    def greet_spectrum(i, carry):
+        signal(spectrum_device(SLOTS * (1 - part) + i))
+        return carry
+    lax.fori_loop(0, SLOTS, greet_spectrum, 0, unroll=8)
     greet_all(jnp.where(special, 8, 4), line_device)
 
     @pl.when(y_device)
@@ -194,8 +213,7 @@
              (w, lax.rem(n + 1, NARROW)), (w, lax.rem(n + NARROW - 1, NARROW))]
     for device in sides:
         greet(device)
-    on_both = half == part
-    expected = (128 - 2 * jnp.where(on_both, 1, 0)
+    expected = (96 - jnp.where(on_both, 1, 0)
                 + jnp.where(special, 8, 4) - jnp.where(w <= SLOTS, 1, 0)
                 + jnp.where(y_device, 7, 0) + 4)
 
@@ -242,21 +260,38 @@
         local(ref, ref, sem).wait()
 
 
-    def spectra_start():
+    def columns(chunk):
+        return pl.ds(512 * chunk[0], 512 * len(chunk))
+
+    def scatter(count, first, src_row, src, dst, dst_row, dump, cols, send, recv, device):
+        def copy(i):
+            return pltpu.make_async_remote_copy(
+                src.at[pl.ds(src_row(i), 1), cols], dst.at[pl.ds(dst_row, 1), cols], send, recv,
+                device_id=device(i), device_id_type=MESH)
+
         def go(step, carry):
-            i = lax.rem(w + step, 64)
-            put(s1.at[pl.ds(lax.rem(i, SLOTS), 1)], r1.at[pl.ds(w, 1)], spare_row.at[pl.ds(0, 1)],
-                send1, recv1, spectrum_device(i))
-            return carry
-        lax.fori_loop(0, 64, go, 0)
-
-    def bricks_start():
-        def go(step, carry):
-            i = lax.rem(w + step, 64)
-            put(s4.at[pl.ds(i, 1)], r4.at[pl.ds(SLOTS * half + slot, 1)], spare_row.at[pl.ds(8, 1)],
-                send4, recv4, brick_device(i))
-            return carry
-        lax.fori_loop(0, 64, go, 0)
+            copy(lax.rem(first + step, count)).start()
+            return carry
+
+        lax.fori_loop(1, count, go, 0, unroll=UNROLL)
+
+        @pl.when(on_both)
+        def _():
+            own = src.at[pl.ds(src_row(first), 1), cols]
+            local(own, dst.at[pl.ds(dst_row, 1), cols], recv).start()
+            local(own, spare_row.at[pl.ds(dump, 1), cols], send).start()
+
+        @pl.when(jnp.logical_not(on_both))
+        def _():
+            copy(first).start()
+
+    def spectra_start(g, chunk):
+        scatter(64, SLOTS * half + slot, lambda i: lax.rem(i, SLOTS), s1, r1, w, 0, columns(chunk),
+                send1.at[g], recv1.at[g], spectrum_device)
+
+    def bricks_start(g, chunk):
+        scatter(64, w, lambda i: i, s4, r4, SLOTS * half + slot, 8, columns(chunk),
+                send4.at[g], recv4.at[g], brick_device)
 
     def lines_start(c):
         def go(i, carry):
@@ -286,7 +321,8 @@
             (hx_send.at[0], hx.at[0]), (hx_send.at[1], hx.at[1]),
             (hy_send.at[0], hy.at[0]), (hy_send.at[1], hy.at[1])))]
 
-    spectra_start()
+    for g, chunk in enumerate(S1_CHUNKS):
+        spectra_start(g, chunk)
     for copy in halo:
         copy.start()
     for copy in loads[4:]:
@@ -330,10 +366,6 @@
             store(mm((square[0, 0], square[0, 1]), split(other)), 4)
 
         lines_start(c)
-
-    done(r1, recv1)
-    for c in range(3):
-        x_forward(c)
 
     def y_forward(c):
         done(r2.at[c], recv2.at[c])
@@ -359,6 +391,20 @@
             return carry
 
         lax.fori_loop(0, 2, multiply, 0)
+
+    def ahead(chunk):
+        @pl.when(y_device)
+        def _():
+            for c in chunk:
+                y_forward(c)
+
+    for g, chunk in enumerate(S1_CHUNKS):
+        done(r1.at[:, columns(chunk)], recv1.at[g])
+        for c in chunk:
+            x_forward(c)
+        if g:
+            ahead(S1_CHUNKS[g - 1])
+    ahead(S1_CHUNKS[-1])
 
     def y_inverse(c):
         a, b, d = ROWS_OF[c]
@@ -416,10 +462,12 @@
         def _():
             store(transform(4)[:NX] * 0.5, 256)
 
+        for g, chunk in enumerate(S4_CHUNKS):
+            if c == chunk[-1]:
+                bricks_start(g, chunk)
+
     @pl.when(y_device)
     def _():
-        for c in range(3):
-            y_forward(c)
         y_inverse(0)
         y_inverse(1)
 
@@ -431,7 +479,6 @@
 
     x_inverse(1)
     x_inverse(2)
-    bricks_start()
 
     for copy in halo:
         copy.wait()
@@ -468,8 +515,10 @@
                 field = field + 2.0 * anis / sat * here[2]
             base[c, xx] = field
 
-    done(r4, recv4)
     for c in range(3):
+        for g, chunk in enumerate(S4_CHUNKS):
+            if c == chunk[0]:
+                done(r4.at[:, columns(chunk)], recv4.at[g])
         got = r4[:, 512 * c:512 * c + 512]
         rhs = jnp.concatenate([got[:, 0:256], got[:, 256:512]], 0)
         out = mm((zi[0], zi[1]), split(rhs))
@@ -486,8 +535,10 @@
         for c in range(3):
             rate_out[c, rows, :] = -(torque[c] + a * second[c]) / (1.0 + a * a)
 
-    done(r1, send1)
-    done(s4, send4)
+    for g, chunk in enumerate(S1_CHUNKS):
+        done(r1.at[:, columns(chunk)], send1.at[g])
+    for g, chunk in enumerate(S4_CHUNKS):
+        done(s4.at[:, columns(chunk)], send4.at[g])
     for c in range(3):
         done_blocks(s2.at[c], send2.at[c])
 
@@ -537,7 +588,7 @@
             pltpu.VMEM((6, ROWS, 256), F32),
         ]
         + [dma((8,))]
-        + [dma] * 2 + [dma((3,))] * 4 + [dma] * 2
+        + [dma((3,))] * 8
         + [dma((4,)), dma((4,))],
         compiler_params=pltpu.CompilerParams(
             collective_id=0, has_side_effects=True, vmem_limit_bytes=56 * 2**20

time: 88.5 us -> 81.4 us (0.920)
  the two profiles are of different devices: /device:TPU:57 before, /device:TPU:33 now
where the time goes in v2:
time: 81.4 us; the launch traced here: 81.3 us
  Pallas kernels  78.4 us (96%)
  local copies, waits for them, and re-layouts  2.22 us (3%)
    pallas_call x1, Pallas kernels, shards(): pl.pallas_call(kernel, out_shape=(out, out), in_specs=[hbm] * 3 + [smem]...  78.4 us
    unnamed x4, local copies, waits for them, and re-layouts  2.22 us

profile of v2, /device:TPU:33, one launch (start us, length us, event | category | flops | bytes accessed | tf_op | source)
XLA Modules:
  0.0 81.3 jit_solution(16054086175457302408)
XLA Ops:
  0.6 78.4 %shard_map.131 = (f32[3,64,128]{2,1,0:T(8,128)}, f32[3,64,128]{2,1,0:T(8,128)}) custom-call(f32[3,64,128]{2,1,0:T(8,128)} %bitcast.7, s32[64,128]{1,0:T(8,128)} %bitcast.10, s32[64,128]{1,0:T(8,128)} %bitcast.11, f32[4]{0:T(128)} %satur.1, f32[4]{0:T(128)} %aniso.1, f32[4]{0:T(128)} %damp.1, f32[3]{0:T(128)} %applied.1, bf16[6,32,2048]{2,1,0:T(8,128)(2,1)} %bitcast.6, ...), custom_call_target="tpu_custom_call" | custom-call | tf_op jit(solution)/shard_map/pallas_call | solution.py:564
  79.0 0.0 copy-start
  79.0 1.6 %copy.16 = f32[3,32,2,128]{3,2,1,0:T(2,128)} copy(f32[3,32,2,128]{3,2,1,0:T(2,128)} %bitcast.9) | data formatting | bytes 196608
  80.6 0.0 copy-done
  80.6 0.6 copy.17
Async XLA Ops:
  79.0 1.6 %copy-start = (f32[3,64,128]{2,1,0:T(8,128)S(1)}, f32[3,64,128]{2,1,0:T(8,128)}, u32[]{:S(2)}) copy-start(f32[3,64,128]{2,1,0:T(8,128)} %get-tuple-element.5) | copy-start | bytes 294916

commit v3 on v2

--- a/solution.py
+++ b/solution.py
@@ -231,6 +231,89 @@
         s1[:, 512 * c:512 * c + 256] = out[:SLOTS]
         s1[:, 512 * c + 256:512 * c + 512] = out[SLOTS:]
 
+    pl.semaphore_wait(barrier, expected)
+
+    def local(src, dst, sem):
+        return pltpu.make_async_copy(src, dst, sem)
+
+    def put(src, dst, dump, send, recv, device):
+        @pl.when(is_me(device))
+        def _():
+            local(src, dst, recv).start()
+            local(src, dump, send).start()
+
+        @pl.when(jnp.logical_not(is_me(device)))
+        def _():
+            pltpu.make_async_remote_copy(
+                src, dst, send, recv, device_id=device, device_id_type=MESH).start()
+
+    def done(ref, sem):
+        local(ref, ref, sem).wait()
+
+
+    def columns(chunk):
+        return pl.ds(512 * chunk[0], 512 * len(chunk))
+
+    def scatter(count, first, src_row, src, dst, dst_row, dump, cols, send, recv, device):
+        def copy(i):
+            return pltpu.make_async_remote_copy(
+                src.at[pl.ds(src_row(i), 1), cols], dst.at[pl.ds(dst_row, 1), cols], send, recv,
+                device_id=device(i), device_id_type=MESH)
+
+        def go(step, carry):
+            copy(lax.rem(first + step, count)).start()
+            return carry
+
+        lax.fori_loop(1, count, go, 0, unroll=UNROLL)
+
+        @pl.when(on_both)
+        def _():
+            own = src.at[pl.ds(src_row(first), 1), cols]
+            local(own, dst.at[pl.ds(dst_row, 1), cols], recv).start()
+            local(own, spare_row.at[pl.ds(dump, 1), cols], send).start()
+
+        @pl.when(jnp.logical_not(on_both))
+        def _():
+            copy(first).start()
+
+    def spectra_start(g, chunk):
+        scatter(64, SLOTS * half + slot, lambda i: lax.rem(i, SLOTS), s1, r1, w, 0, columns(chunk),
+                send1.at[g], recv1.at[g], spectrum_device)
+
+    def bricks_start(g, chunk):
+        scatter(64, w, lambda i: i, s4, r4, SLOTS * half + slot, 8, columns(chunk),
+                send4.at[g], recv4.at[g], brick_device)
+
+    def lines_start(c):
+        def go(i, carry):
+            put(s2.at[c, i], r2.at[c, 4 * part + column], spare.at[c], send2.at[c], recv2.at[c], line_device(i))
+            return carry
+        lax.fori_loop(0, jnp.where(special, 8, 4), go, 0)
+
+    def planes_start(c):
+        def go(i, carry):
+            put(s3.at[c, i], r3.at[c, column + jnp.where(w == SLOTS, 4, 0)], spare.at[3 + c],
+                send3.at[c], recv3.at[c], plane_device(i))
+            return carry
+        lax.fori_loop(0, 8, go, 0)
+
+    def done_blocks(ref, sem):
+        @pl.when(special)
+        def _():
+            done(ref, sem)
+
+        @pl.when(jnp.logical_not(special))
+        def _():
+            done(ref.at[pl.ds(0, 4)], sem)
+
+    halo = [pltpu.make_async_remote_copy(
+        src, dst, hsend.at[i], hrecv.at[i], device_id=sides[i], device_id_type=MESH)
+        for i, (src, dst) in enumerate((
+            (hx_send.at[0], hx.at[0]), (hx_send.at[1], hx.at[1]),
+            (hy_send.at[0], hy.at[0]), (hy_send.at[1], hy.at[1])))]
+
+    for g, chunk in enumerate(S1_CHUNKS):
+        spectra_start(g, chunk)
     lane = lax.broadcasted_iota(jnp.int32, (NZ, LANES), 1)
     for xx in range(2):
         for c in range(3):
@@ -240,91 +323,6 @@
             hy_send[side, NZ * xx:NZ * xx + NZ, :] = jnp.where(
                 lane == 0, cols[0], jnp.where(lane == 1, cols[1], cols[2]))
 
-    pl.semaphore_wait(barrier, expected)
-
-    def local(src, dst, sem):
-        return pltpu.make_async_copy(src, dst, sem)
-
-    def put(src, dst, dump, send, recv, device):
-        @pl.when(is_me(device))
-        def _():
-            local(src, dst, recv).start()
-            local(src, dump, send).start()
-
-        @pl.when(jnp.logical_not(is_me(device)))
-        def _():
-            pltpu.make_async_remote_copy(
-                src, dst, send, recv, device_id=device, device_id_type=MESH).start()
-
-    def done(ref, sem):
-        local(ref, ref, sem).wait()
-
-
-    def columns(chunk):
-        return pl.ds(512 * chunk[0], 512 * len(chunk))
-
-    def scatter(count, first, src_row, src, dst, dst_row, dump, cols, send, recv, device):
-        def copy(i):
-            return pltpu.make_async_remote_copy(
-                src.at[pl.ds(src_row(i), 1), cols], dst.at[pl.ds(dst_row, 1), cols], send, recv,
-                device_id=device(i), device_id_type=MESH)
-
-        def go(step, carry):
-            copy(lax.rem(first + step, count)).start()
-            return carry
-
-        lax.fori_loop(1, count, go, 0, unroll=UNROLL)
-
-        @pl.when(on_both)
-        def _():
-            own = src.at[pl.ds(src_row(first), 1), cols]
-            local(own, dst.at[pl.ds(dst_row, 1), cols], recv).start()
-            local(own, spare_row.at[pl.ds(dump, 1), cols], send).start()
-
-        @pl.when(jnp.logical_not(on_both))
-        def _():
-            copy(first).start()
-
-    def spectra_start(g, chunk):
-        scatter(64, SLOTS * half + slot, lambda i: lax.rem(i, SLOTS), s1, r1, w, 0, columns(chunk),
-                send1.at[g], recv1.at[g], spectrum_device)
-
-    def bricks_start(g, chunk):
-        scatter(64, w, lambda i: i, s4, r4, SLOTS * half + slot, 8, columns(chunk),
-                send4.at[g], recv4.at[g], brick_device)
-
-    def lines_start(c):
-        def go(i, carry):
-            put(s2.at[c, i], r2.at[c, 4 * part + column], spare.at[c], send2.at[c], recv2.at[c], line_device(i))
-            return carry
-        lax.fori_loop(0, jnp.where(special, 8, 4), go, 0)
-
-    def planes_start(c):
-        def go(i, carry):
-            put(s3.at[c, i], r3.at[c, column + jnp.where(w == SLOTS, 4, 0)], spare.at[3 + c],
-                send3.at[c], recv3.at[c], plane_device(i))
-            return carry
-        lax.fori_loop(0, 8, go, 0)
-
-    def done_blocks(ref, sem):
-        @pl.when(special)
-        def _():
-            done(ref, sem)
-
-        @pl.when(jnp.logical_not(special))
-        def _():
-            done(ref.at[pl.ds(0, 4)], sem)
-
-    halo = [pltpu.make_async_remote_copy(
-        src, dst, hsend.at[i], hrecv.at[i], device_id=sides[i], device_id_type=MESH)
-        for i, (src, dst) in enumerate((
-            (hx_send.at[0], hx.at[0]), (hx_send.at[1], hx.at[1]),
-            (hy_send.at[0], hy.at[0]), (hy_send.at[1], hy.at[1])))]
-
-    for g, chunk in enumerate(S1_CHUNKS):
-        spectra_start(g, chunk)
-    for copy in halo:
-        copy.start()
     for copy in loads[4:]:
         copy.wait()
 
@@ -383,14 +381,14 @@
                 work[at, 128:256] = re * sin + im * cos
             return carry
 
-        lax.fori_loop(0, 4, go, 0)
+        lax.fori_loop(0, 4, go, 0, unroll=2)
 
         def multiply(t, carry):
             rows = pl.ds(pl.multiple_of(256 * t, 256), 256)
             spectra[c, rows, :] = mm(split(work[rows, :]), (square[2, 0], square[2, 1]))
             return carry
 
-        lax.fori_loop(0, 2, multiply, 0)
+        lax.fori_loop(0, 2, multiply, 0, unroll=True)
 
     def ahead(chunk):
         @pl.when(y_device)
@@ -404,6 +402,8 @@
             x_forward(c)
         if g:
             ahead(S1_CHUNKS[g - 1])
+    for copy in halo:
+        copy.start()
     ahead(S1_CHUNKS[-1])
 
     def y_inverse(c):
@@ -417,7 +417,7 @@
             work[rows, :] = mm(split(jnp.concatenate(field, 1)), (square[3, 0], square[3, 1]))
             return carry
 
-        lax.fori_loop(0, 2, multiply, 0)
+        lax.fori_loop(0, 2, multiply, 0, unroll=True)
 
         def go(t, carry):
             u = []
@@ -435,7 +435,7 @@
                 s3[c, j, rows, 128:256] = even[j][1] + o[1]
             return carry
 
-        lax.fori_loop(0, 4, go, 0)
+        lax.fori_loop(0, 4, go, 0, unroll=2)
         planes_start(c)
 
     def x_inverse(c):
@@ -468,15 +468,10 @@
 
     @pl.when(y_device)
     def _():
-        y_inverse(0)
-        y_inverse(1)
+        for c in range(3):
+            y_inverse(c)
 
     x_inverse(0)
-
-    @pl.when(y_device)
-    def _():
-        y_inverse(2)
-
     x_inverse(1)
     x_inverse(2)
 

time: 81.4 us -> 80.2 us (0.985)
  the two profiles are of different devices: /device:TPU:33 before, /device:TPU:57 now
where the time goes in v3:
time: 80.2 us; the launch traced here: 80.1 us
  Pallas kernels  77.2 us (96%)
  local copies, waits for them, and re-layouts  2.22 us (3%)
    pallas_call x1, Pallas kernels, shards(): pl.pallas_call(kernel, out_shape=(out, out), in_specs=[hbm] * 3 + [smem]...  77.2 us
    unnamed x4, local copies, waits for them, and re-layouts  2.22 us

profile of v3, /device:TPU:57, one launch (start us, length us, event | category | flops | bytes accessed | tf_op | source)
XLA Modules:
  0.0 80.1 jit_solution(7215966496345793051)
XLA Ops:
  0.6 77.2 %shard_map.131 = (f32[3,64,128]{2,1,0:T(8,128)}, f32[3,64,128]{2,1,0:T(8,128)}) custom-call(f32[3,64,128]{2,1,0:T(8,128)} %bitcast.7, s32[64,128]{1,0:T(8,128)} %bitcast.10, s32[64,128]{1,0:T(8,128)} %bitcast.11, f32[4]{0:T(128)} %satur.1, f32[4]{0:T(128)} %aniso.1, f32[4]{0:T(128)} %damp.1, f32[3]{0:T(128)} %applied.1, bf16[6,32,2048]{2,1,0:T(8,128)(2,1)} %bitcast.6, ...), custom_call_target="tpu_custom_call" | custom-call | tf_op jit(solution)/shard_map/pallas_call | solution.py:559
  77.8 0.0 copy-start
  77.8 1.6 %copy.16 = f32[3,32,2,128]{3,2,1,0:T(2,128)} copy(f32[3,32,2,128]{3,2,1,0:T(2,128)} %bitcast.9) | data formatting | bytes 196608
  79.4 0.0 copy-done
  79.4 0.6 copy.17
Async XLA Ops:
  77.8 1.6 %copy-start = (f32[3,64,128]{2,1,0:T(8,128)S(1)}, f32[3,64,128]{2,1,0:T(8,128)}, u32[]{:S(2)}) copy-start(f32[3,64,128]{2,1,0:T(8,128)} %get-tuple-element.5) | copy-start | bytes 294916

commit v4 on v3

--- a/solution.py
+++ b/solution.py
@@ -154,7 +154,7 @@
     loads = [pltpu.make_async_copy(a, b, load.at[i]) for i, (a, b) in enumerate((
         (spin_hbm, spin), (region_hbm, region), (material_hbm, material), (zf_hbm, zf),
         (spec_hbm, spec), (square_hbm, square), (twist_hbm, twist), (zi_hbm, zi)))]
-    for copy in loads:
+    for copy in loads[:4]:
         copy.start()
 
     def spectrum_device(i):
@@ -225,11 +225,14 @@
         satcell[xx] = pick(material[rows, :], satur)
         for c in range(3):
             direction[c, xx] = spin[c, rows, :] * mag
-    for c in range(3):
+    def z_forward_part(c):
         moment = jnp.concatenate([direction[c, xx] * satcell[xx] for xx in range(2)], 1)
         out = mm((zf[0], zf[1]), split(moment))
         s1[:, 512 * c:512 * c + 256] = out[:SLOTS]
         s1[:, 512 * c + 256:512 * c + 512] = out[SLOTS:]
+
+    for c in S1_CHUNKS[0]:
+        z_forward_part(c)
 
     pl.semaphore_wait(barrier, expected)
 
@@ -313,7 +316,13 @@
             (hy_send.at[0], hy.at[0]), (hy_send.at[1], hy.at[1])))]
 
     for g, chunk in enumerate(S1_CHUNKS):
+        if g:
+            for c in chunk:
+                z_forward_part(c)
         spectra_start(g, chunk)
+        if g == 0:
+            for copy in loads[4:]:
+                copy.start()
     lane = lax.broadcasted_iota(jnp.int32, (NZ, LANES), 1)
     for xx in range(2):
         for c in range(3):

time: 80.2 us -> 80.1 us (level)
  no operation moved by 1% of the time
where the time goes in v4:
time: 80.1 us; the launch traced here: 79.9 us
  Pallas kernels  77.1 us (96%)
  local copies, waits for them, and re-layouts  2.22 us (3%)
    pallas_call x1, Pallas kernels, shards(): pl.pallas_call(kernel, out_shape=(out, out), in_specs=[hbm] * 3 + [smem]...  77.1 us
    unnamed x4, local copies, waits for them, and re-layouts  2.22 us

profile of v4, /device:TPU:57, one launch (start us, length us, event | category | flops | bytes accessed | tf_op | source)
XLA Modules:
  0.0 79.9 jit_solution(1835767345237938538)
XLA Ops:
  0.6 77.1 %shard_map.131 = (f32[3,64,128]{2,1,0:T(8,128)}, f32[3,64,128]{2,1,0:T(8,128)}) custom-call(f32[3,64,128]{2,1,0:T(8,128)} %bitcast.7, s32[64,128]{1,0:T(8,128)} %bitcast.10, s32[64,128]{1,0:T(8,128)} %bitcast.11, f32[4]{0:T(128)} %satur.1, f32[4]{0:T(128)} %aniso.1, f32[4]{0:T(128)} %damp.1, f32[3]{0:T(128)} %applied.1, bf16[6,32,2048]{2,1,0:T(8,128)(2,1)} %bitcast.6, ...), custom_call_target="tpu_custom_call" | custom-call | tf_op jit(solution)/shard_map/pallas_call | solution.py:568
  77.7 0.0 copy-start
  77.7 1.6 %copy.16 = f32[3,32,2,128]{3,2,1,0:T(2,128)} copy(f32[3,32,2,128]{3,2,1,0:T(2,128)} %bitcast.9) | data formatting | bytes 196608
  79.3 0.0 copy-done
  79.3 0.6 copy.17
Async XLA Ops:
  77.7 1.6 %copy-start = (f32[3,64,128]{2,1,0:T(8,128)S(1)}, f32[3,64,128]{2,1,0:T(8,128)}, u32[]{:S(2)}) copy-start(f32[3,64,128]{2,1,0:T(8,128)} %get-tuple-element.5) | copy-start | bytes 294916
